TPU v7x, 32 devices: a whole 2x2x4 slice. The times are simulated.
32 devices in a mesh: tm: 16 (over z, y, x), pad: 2 (over core).
Axes of the slice: x: 2, y: 2, z: 4, core: 2. Of those that a mesh axis runs over, the one named last changes fastest.
Arguments:
- charge: float32 [2, 8192], P('pad', 'tm'), may hold values from 0.3 to 3
- pad_row: int32 [2, 8192], P('pad', 'tm'), may hold values from 0 to 39
- pad_column: int32 [2, 8192], P('pad', 'tm'), may hold values from 0 to 65
- time_bin: int32 [2, 8192], P('pad', 'tm'), may hold values from 0 to 1023
- slab_owner: int32 [2, 8192, 1], P('pad', 'tm'), may hold values from 0 to 15; in each aligned block of 512 rows (0 to 511, 512 to 1023, ..., all dimensions but the last counted through in order) at most 48 rows name the same one
- block_count: int32 [2, 64], P('pad', 'tm'), may hold values from 1 to 128
- shaping: float32 [1024], replicated, may hold values from 0.02 to 1
- response: float32 [3, 3], replicated, may hold values from 0.05 to 1
Outputs:
- signal: float32 [80, 66, 16384], P('pad', None, 'tm')
Inputs may be any that keep to these rules, and one draw needn't show every extreme that they name: `slab_owner`: among the cluster rows of one device, at most 48 name the same time slab, a bound that some of them reach. Only the first block_count rows of each block of 128 cluster rows hold clusters.
All inputs are finite; a program needn't handle non-finite values.
Results may differ from a plain program's by a relative error of at most 0.0003.
Values sent between devices are 32-bit elements; how exact they have to be, the bound alone decides.
No kernel may reach another device: no remote copies, remote signals or barrier semaphores. Data moves between devices by JAX's collectives and lax.ppermute only.
A program may use at most 128 MiB of HBM per device.

v0:
```python
import functools

import jax
import jax.numpy as jnp
from jax import lax
from jax.experimental import pallas as pl
from jax.experimental.pallas import tpu as pltpu
from jax.sharding import PartitionSpec as P

PROWS = 80
PPR = 66
T_DEV = 1024

LANES = 128
GROUP = 6
WINDOW = 80
NT = (((1,), (1,)), ((), ()))


def iota(shape, dim):
    return lax.broadcasted_iota(jnp.int32, shape, dim)


def pieces(x):
    high = x.astype(jnp.bfloat16).astype(jnp.float32)
    rest = x - high
    middle = rest.astype(jnp.bfloat16).astype(jnp.float32)
    low = rest - middle
    return jnp.concatenate([high, middle, low, jnp.zeros_like(x)], axis=0).astype(jnp.bfloat16)


def joined(x):
    return (x[0:4] + x[4:8]) + x[8:12]


def running():
    source, lane = iota((LANES, 2 * LANES), 0), iota((LANES, 2 * LANES), 1)
    return jnp.where((lane >= LANES) | (source <= lane), 1.0, 0.0).astype(jnp.bfloat16)


def route_kernel(slabs, pads, row_count, room, group_ref, *refs):
    sources, (out_ref,), (sems,), targets = refs[:6], refs[6:7], refs[7:8], refs[8:]
    copies = [pltpu.make_async_copy(*pair, sems.at[k]) for k, pair in enumerate(zip(sources, targets))]
    for copy in copies:
        copy.start()
    for copy in copies:
        copy.wait()
    count_ref, charge_ref, row_ref, column_ref, bin_ref, slab_ref = targets
    rows = charge_ref.shape[1]
    blocks = rows // LANES
    group = group_ref[0]
    sums = running()
    slab_ids = iota((slabs, LANES), 0)
    lane = iota((1, LANES), 1)
    before = jnp.zeros((slabs, LANES), jnp.float32)
    slots, values = [], []
    for block in range(blocks):
        at = pl.ds(block * LANES, LANES)
        live = lane < count_ref[0, block]
        slab = jnp.where(live, slab_ref[:, at], -1)
        marks = jnp.where(slab_ids == slab, 1.0, 0.0)
        totals = jnp.dot(marks.astype(jnp.bfloat16), sums, preferred_element_type=jnp.float32)
        rank = jnp.sum(marks * (totals[:, :LANES] + before), axis=0, keepdims=True)
        before = before + totals[:, LANES:]
        slots.append(jnp.where(live, slab * room + rank.astype(jnp.int32) - 1, -1))
        values.append(
            jnp.concatenate(
                [
                    charge_ref[:, at],
                    (row_ref[:, at] + 2).astype(jnp.float32),
                    column_ref[:, at].astype(jnp.float32),
                    bin_ref[:, at].astype(jnp.float32),
                ],
                axis=0,
            )
        )
    payload = pieces(jnp.concatenate(values, axis=1))
    slot = jnp.concatenate(slots, axis=1)
    hits = jnp.where(iota((slabs * room, rows), 0) == slot, 1.0, 0.0).astype(jnp.bfloat16)
    placed = joined(lax.dot_general(payload, hits, NT, preferred_element_type=jnp.float32))
    feature, half = iota((4, LANES), 0), iota((4, LANES), 1) // room
    for slab in range(slabs):
        tile = placed[:, slab // 2 * LANES : slab // 2 * LANES + LANES]
        if slab % 2 == 0:
            other = placed[:, (slab // 2 - 1) * LANES : slab // 2 * LANES] if slab else jnp.zeros_like(tile)
            tile = jnp.where(half == 0, tile, other)
        tile = jnp.where((feature == 3) & (half != slab % 2), tile - T_DEV, tile)
        top = jnp.where(feature == 1, jnp.where(tile == row_count + 1, 1.0, 0.0), tile)
        bottom = jnp.where(feature == 1, jnp.where(tile == 2, row_count + 2.0, 0.0), tile)
        for pad in range(pads):
            apart = pad - group
            out_ref[slab * pads + pad] = jnp.where(
                apart == 0, tile, jnp.where(apart == 1, top, jnp.where(apart == -1, bottom, 0.0))
            )


def signal_kernel(
    row_count,
    response_ref,
    slots_ref,
    shaping_ref,
    out_ref,
    payload_ref,
    place_ref,
    marks_ref,
    totals_ref,
    table_ref,
    feature_ref,
    time_ref,
    first_ref,
    stage_ref,
    high_ref,
    low_ref,
    result_ref,
    time_smem,
    first_smem,
    time_sem,
    first_sem,
    out_sems,
):
    count = slots_ref.shape[0]
    step = min(count, 32)
    parts = count // step
    buckets = first_ref.shape[0]
    chunks = T_DEV // LANES

    sums = running()
    bucket_ids = iota((buckets, LANES), 0).astype(jnp.float32)

    def mark(part, earlier):
        for k in range(step):
            block = part * step + k
            slot = slots_ref[block]
            payload_ref[block] = pieces(slot)
            column = slot[2:3] + 1.0
            block_at = jnp.floor((column + 0.5) * (1.0 / GROUP))
            inner = jnp.where(column - block_at * GROUP > 1.5, 1.0, 0.0)
            bucket = jnp.where(slot[1:2] > 0.5, 2.0 * block_at + inner, -1.0)
            marks_ref[pl.ds(block * buckets, buckets), :] = jnp.where(bucket_ids == bucket, 1.0, 0.0)
            earlier = earlier + jnp.where((bucket >= 0.0) & (bucket < bucket_ids), 1.0, 0.0)
        return earlier

    earlier = lax.fori_loop(0, parts, mark, jnp.zeros((buckets, LANES), jnp.float32))
    first = jnp.dot(earlier.astype(jnp.bfloat16), sums, preferred_element_type=jnp.float32)[:, LANES:]
    first_ref[...] = first.astype(jnp.int32)
    first_copy = pltpu.make_async_copy(first_ref, first_smem, first_sem)
    first_copy.start()

    def number(part, before):
        at = pl.ds(part * step * buckets, step * buckets)
        totals_ref[...] = jnp.dot(marks_ref[at, :].astype(jnp.bfloat16), sums, preferred_element_type=jnp.float32)
        for k in range(step):
            block = part * step + k
            marks = marks_ref[pl.ds(block * buckets, buckets), :]
            within = totals_ref[k * buckets : (k + 1) * buckets, :LANES]
            place_ref[block] = jnp.sum(marks * (within + before), axis=0, keepdims=True)
            before = before + totals_ref[k * buckets : (k + 1) * buckets, LANES:]
        return before

    lax.fori_loop(0, parts, number, first)
    total = jnp.max(first).astype(jnp.int32)
    filled = (total + LANES - 1) // LANES

    position = iota((LANES, LANES), 0).astype(jnp.float32) + 1.0

    def sort(chunk, carry):
        wanted = position + (chunk * LANES).astype(jnp.float32)

        def add(part, accum):
            hits = [
                jnp.where(place_ref[part * step + k] == wanted, 1.0, 0.0).astype(jnp.bfloat16)
                for k in range(step)
            ]
            held = [payload_ref[part * step + k] for k in range(step)]
            return accum + lax.dot_general(
                jnp.concatenate(held, axis=1),
                jnp.concatenate(hits, axis=1),
                NT,
                preferred_element_type=jnp.float32,
            )

        placed = joined(lax.fori_loop(0, parts, add, jnp.zeros((16, LANES), jnp.float32)))
        feature_ref[chunk] = placed
        time_ref[pl.ds(chunk, 1), :] = placed[3:4].astype(jnp.int32)
        return carry

    lax.fori_loop(0, filled, sort, 0)
    feature_ref[filled] = jnp.zeros((4, LANES), jnp.float32)
    time_copy = pltpu.make_async_copy(time_ref, time_smem, time_sem)
    time_copy.start()

    kernel = shaping_ref[...]
    lane, sublane = iota((chunks, LANES), 1), iota((chunks, LANES), 0)
    moved = jnp.concatenate([jnp.zeros((1, LANES), jnp.float32), kernel[: chunks - 1]], axis=0)
    tail = jnp.where(sublane == 0, kernel[chunks - 1 : chunks], 0.0)
    for shift in range(LANES):
        inside = lane < LANES - shift
        base = shift * 3 * chunks
        table_ref[base : base + chunks, :] = jnp.zeros((chunks, LANES), jnp.float32)
        table_ref[base + chunks : base + 2 * chunks, :] = pltpu.roll(jnp.where(inside, kernel, moved), shift, 1)
        table_ref[base + 2 * chunks : base + 3 * chunks, :] = pltpu.roll(jnp.where(inside, 0.0, tail), shift, 1)
    time_copy.wait()
    first_copy.wait()

    stride = stage_ref.shape[0] // chunks

    def shape(chunk, carry):
        def eight(eighth, carry):
            for k in range(8):
                index = eighth * 8 + k
                time = time_smem[chunk, index]
                begin = (time & (LANES - 1)) * (3 * chunks) + chunks - (time >> 7)
                stage_ref[pl.ds(index, chunks, stride=stride), :] = table_ref[pl.ds(begin, chunks), :]
            return carry

        lax.fori_loop(0, LANES // 8, eight, 0)
        at = pl.ds(pl.multiple_of(chunk * LANES, LANES), LANES)
        for c in range(chunks):
            value = stage_ref[c * stride : c * stride + LANES, :]
            high = value.astype(jnp.bfloat16)
            high_ref[c, at, :] = high
            low_ref[c, at, :] = (value - high.astype(jnp.float32)).astype(jnp.bfloat16)
        return carry

    lax.fori_loop(0, filled, shape, 0)
    beyond = pl.ds(pl.multiple_of(filled * LANES, LANES), LANES)
    for c in range(chunks):
        high_ref[c, beyond, :] = jnp.zeros((LANES, LANES), jnp.bfloat16)
        low_ref[c, beyond, :] = jnp.zeros((LANES, LANES), jnp.bfloat16)

    wide = 2 * LANES
    spot = iota((1, wide), 1)
    padded = -(-row_count // 8) * 8
    row = iota((padded, wide), 0)

    def weights(group, begin):
        chunk, offset = begin // LANES, begin % LANES
        window = jnp.concatenate([feature_ref[chunk], feature_ref[chunk + 1]], axis=1)
        window = pltpu.roll(jnp.concatenate([window, window], axis=0), wide - offset, 1)
        window = jnp.where(
            spot < WINDOW,
            window,
            jnp.where(spot < 2 * WINDOW, pltpu.roll(window, WINDOW, 1), pltpu.roll(window, 2 * WINDOW, 1)),
        )
        charge = jnp.where(spot < 3 * WINDOW, window[0:1], 0.0)
        below, column = window[1:2].astype(jnp.int32) - 1 - row, window[2:3].astype(jnp.int32)
        masks = [below == a for a in range(3)]
        blocks = []
        for k in range(GROUP):
            beside = column - (group * GROUP + k - 1)
            terms = []
            for a in range(3):
                gain = jnp.where(
                    beside == 0,
                    response_ref[a, 0],
                    jnp.where(beside == 1, response_ref[a, 1], jnp.where(beside == 2, response_ref[a, 2], 0.0)),
                )
                term = charge * gain
                high = term.astype(jnp.bfloat16).astype(jnp.float32)
                terms.append(jnp.where(spot < 2 * WINDOW, high, term - high))
            blocks.append(
                jnp.where(masks[0], terms[0], jnp.where(masks[1], terms[1], jnp.where(masks[2], terms[2], 0.0)))
            )
        return jnp.concatenate(blocks, axis=0).astype(jnp.bfloat16)

    def product(group, begin, c, held):
        at = pl.ds(pl.multiple_of(begin, 16), WINDOW)
        filler = jnp.zeros((wide - 3 * WINDOW, LANES), jnp.bfloat16)
        high = [high_ref[k, at, :] for k in (c, c + 1)]
        low = [low_ref[k, at, :] for k in (c, c + 1)]
        columns = [jnp.concatenate([h, l, h, filler], axis=0) for h, l in zip(high, low)]
        values = jnp.dot(held, jnp.concatenate(columns, axis=1), preferred_element_type=jnp.float32)
        return values.reshape(GROUP, padded, wide)[:, :row_count]

    def produce(group, carry):
        start = first_smem[2 * group, 0]
        stop = first_smem[2 * group + 3, 0]
        begin = start // 16 * 16
        pads = pl.ds(group * GROUP, GROUP)
        held = weights(group, begin)
        for c in range(0, chunks, 2):
            result_ref[pads, :, c * LANES : (c + 2) * LANES] = product(group, begin, c, held)

        def more(turn, carry):
            later = begin + turn * WINDOW
            held = weights(group, later)
            for c in range(0, chunks, 2):
                at = (pads, slice(None), slice(c * LANES, (c + 2) * LANES))
                result_ref[at] = result_ref[at] + product(group, later, c, held)
            return carry

        lax.fori_loop(1, (stop - begin + WINDOW - 1) // WINDOW, more, 0)
        pltpu.make_async_copy(result_ref.at[pads], out_ref.at[pads], out_sems.at[group]).start()
        return carry

    groups = PPR // GROUP
    lax.fori_loop(0, groups, produce, 0)

    def finish(group, carry):
        pads = pl.ds(group * GROUP, GROUP)
        pltpu.make_async_copy(result_ref.at[pads], out_ref.at[pads], out_sems.at[group]).wait()
        return carry

    lax.fori_loop(0, groups, finish, 0)


def body(charge, pad_row, pad_column, time_bin, slab_owner, block_count, shaping, response):
    slabs, pads = lax.axis_size("tm"), lax.axis_size("pad")
    rows = charge.shape[1]
    capacity = max(16, 3 * rows // (2 * slabs))
    room = LANES // 2
    assert capacity <= room and slabs % 2 == 0
    row_count = PROWS // pads
    vmem, smem = pl.BlockSpec(memory_space=pltpu.VMEM), pl.BlockSpec(memory_space=pltpu.SMEM)
    sources = (block_count, charge, pad_row, pad_column, time_bin, slab_owner.reshape(1, rows))
    sources = tuple(pltpu.with_memory_space_constraint(source, pltpu.HBM) for source in sources)
    outgoing = pl.pallas_call(
        functools.partial(route_kernel, slabs, pads, row_count, room),
        out_shape=jax.ShapeDtypeStruct((slabs * pads, 4, LANES), jnp.float32),
        in_specs=[smem] + [pl.BlockSpec(memory_space=pltpu.HBM)] * 6,
        out_specs=vmem,
        scratch_shapes=[pltpu.SemaphoreType.DMA((6,)), pltpu.SMEM(block_count.shape, block_count.dtype)]
        + [pltpu.VMEM(source.shape, source.dtype) for source in sources[1:]],
        compiler_params=pltpu.CompilerParams(vmem_limit_bytes=32 * 2**20),
        name="route",
    )(lax.axis_index("pad").astype(jnp.int32).reshape(1), *sources)
    incoming = lax.all_to_all(outgoing, ("tm", "pad"), split_axis=0, concat_axis=0, tiled=True)

    count = slabs * pads
    step = min(count, 32)
    buckets = -(-(2 * PPR // GROUP + 2) // 8) * 8
    most = -(-slabs * 2 * capacity * min(pads, 3) // LANES)
    chunks = T_DEV // LANES
    stride = LANES + 8
    signal = pl.pallas_call(
        functools.partial(signal_kernel, row_count),
        out_shape=jax.ShapeDtypeStruct((PPR, row_count, T_DEV), jnp.float32),
        in_specs=[smem, vmem, vmem],
        out_specs=pl.BlockSpec(memory_space=pl.ANY),
        scratch_shapes=[
            pltpu.VMEM((count, 16, LANES), jnp.bfloat16),
            pltpu.VMEM((count, 1, LANES), jnp.float32),
            pltpu.VMEM((count * buckets, LANES), jnp.float32),
            pltpu.VMEM((step * buckets, 2 * LANES), jnp.float32),
            pltpu.VMEM((LANES * 3 * chunks, LANES), jnp.float32),
            pltpu.VMEM((most + 2, 4, LANES), jnp.float32),
            pltpu.VMEM((most, LANES), jnp.int32),
            pltpu.VMEM((buckets, LANES), jnp.int32),
            pltpu.VMEM((chunks * stride, LANES), jnp.float32),
            pltpu.VMEM((chunks, (most + 1) * LANES, LANES), jnp.bfloat16),
            pltpu.VMEM((chunks, (most + 1) * LANES, LANES), jnp.bfloat16),
            pltpu.VMEM((PPR, row_count, T_DEV), jnp.float32),
            pltpu.SMEM((most, LANES), jnp.int32),
            pltpu.SMEM((buckets, LANES), jnp.int32),
            pltpu.SemaphoreType.DMA,
            pltpu.SemaphoreType.DMA,
            pltpu.SemaphoreType.DMA((PPR // GROUP,)),
        ],
        compiler_params=pltpu.CompilerParams(vmem_limit_bytes=56 * 2**20),
        name="signal",
    )(response, incoming, shaping.reshape(chunks, LANES))
    return signal.transpose(1, 0, 2)


def solution(mesh):
    in_specs = (
        P("pad", "tm"),
        P("pad", "tm"),
        P("pad", "tm"),
        P("pad", "tm"),
        P("pad", "tm", None),
        P("pad", "tm"),
        P(),
        P(),
    )
    out_specs = P("pad", None, "tm")
    return jax.shard_map(body, mesh=mesh, in_specs=in_specs, out_specs=out_specs, check_vma=False)
```

profile of v0, /device:TPU:4, one launch (start us, length us, event | category | flops | bytes accessed | tf_op | source)
XLA Modules:
  0.0 33.0 jit_solution(3229319580369333793)
XLA Ops:
  0.0 1.4 %route.1 = f32[32,4,128]{2,1,0:T(4,128)S(1)} custom-call(s32[1]{0:T(128)} %bitcast.group_ref, s32[1,4]{1,0:T(1,128)} %refs_0_.1, f32[1,512]{1,0:T(1,128)} %refs_1_.1, s32[1,512]{1,0:T(1,128)} %refs_2_.1, s32[1,512]{1,0:T(1,128)} %refs_3_.1, s32[1,512]{1,0:T(1,128)} %refs_4_.1, s32[1,512]{1,0:T(1,128)} %bitcast.5), custom_call_target="tpu_custom_call" | custom-call | tf_op jit(solution)/shard_map/route/pallas_call | solution.py:317
  1.4 12.2 %all_to_all.5.slots_ref = f32[32,4,128]{2,1,0:T(4,128)} all-to-all(f32[32,4,128]{2,1,0:T(4,128)S(1)} %route.1), channel_id=1, replica_groups=mesh['tm'=16,'pad'=2] {'tm','pad'}, dimensions={0} | all-to-all | bytes 131072 | tf_op jit(solution)/shard_map/all_to_all | solution.py:327
  13.7 19.3 %signal.1 = f32[66,40,1024]{2,1,0:T(8,128)} custom-call(f32[3,3]{1,0:T(4,128)} %response_ref.1, f32[32,4,128]{2,1,0:T(4,128)} %all_to_all.5.slots_ref, f32[8,128]{1,0:T(8,128)} %bitcast.4), custom_call_target="tpu_custom_call" | custom-call | tf_op jit(solution)/shard_map/signal/pallas_call | solution.py:335
where the time goes:
time: 33.6 us; the launch traced here: 33 us
  Pallas kernels  20.7 us (62%)
  blocking collectives  12.2 us (36%)
    pallas_call x1, Pallas kernels, body(): pl.pallas_call(functools.partial(signal_kernel, row_count), out_shape=jax...  19.3 us
    all_to_all x1, blocking collectives, body(): lax.all_to_all(outgoing, ('tm', 'pad'), split_axis=0, concat_axis=0, tile...  12.2 us
    pallas_call x1, Pallas kernels, body(): pl.pallas_call(functools.partial(route_kernel, slabs, pads, row_count, ro...  1.43 us

commit v1 on v0

--- a/solution.py
+++ b/solution.py
@@ -13,7 +13,10 @@
 
 LANES = 128
 GROUP = 6
-WINDOW = 80
+BATCHES = (range(0, 6), range(6, 11))
+WEIGH = 11
+ROWS = 128
+SORT = 256
 NT = (((1,), (1,)), ((), ()))
 
 
@@ -106,16 +109,16 @@
     totals_ref,
     table_ref,
     feature_ref,
-    time_ref,
+    begin_ref,
     first_ref,
     stage_ref,
     high_ref,
     low_ref,
+    weight_ref,
     result_ref,
-    time_smem,
+    begin_smem,
     first_smem,
-    time_sem,
-    first_sem,
+    copy_sems,
     out_sems,
 ):
     count = slots_ref.shape[0]
@@ -133,9 +136,9 @@
             slot = slots_ref[block]
             payload_ref[block] = pieces(slot)
             column = slot[2:3] + 1.0
-            block_at = jnp.floor((column + 0.5) * (1.0 / GROUP))
-            inner = jnp.where(column - block_at * GROUP > 1.5, 1.0, 0.0)
-            bucket = jnp.where(slot[1:2] > 0.5, 2.0 * block_at + inner, -1.0)
+            group = jnp.floor((column + 0.5) * (1.0 / GROUP))
+            inside = jnp.where(column - group * GROUP > 1.5, 1.0, 0.0)
+            bucket = jnp.where(slot[1:2] > 0.5, 2.0 * group + inside, -1.0)
             marks_ref[pl.ds(block * buckets, buckets), :] = jnp.where(bucket_ids == bucket, 1.0, 0.0)
             earlier = earlier + jnp.where((bucket >= 0.0) & (bucket < bucket_ids), 1.0, 0.0)
         return earlier
@@ -143,7 +146,7 @@
     earlier = lax.fori_loop(0, parts, mark, jnp.zeros((buckets, LANES), jnp.float32))
     first = jnp.dot(earlier.astype(jnp.bfloat16), sums, preferred_element_type=jnp.float32)[:, LANES:]
     first_ref[...] = first.astype(jnp.int32)
-    first_copy = pltpu.make_async_copy(first_ref, first_smem, first_sem)
+    first_copy = pltpu.make_async_copy(first_ref, first_smem, copy_sems.at[0])
     first_copy.start()
 
     def number(part, before):
@@ -159,18 +162,17 @@
 
     lax.fori_loop(0, parts, number, first)
     total = jnp.max(first).astype(jnp.int32)
-    filled = (total + LANES - 1) // LANES
-
-    position = iota((LANES, LANES), 0).astype(jnp.float32) + 1.0
+    filled = jnp.maximum((total + LANES - 1) // LANES, 1)
+
+    position = iota((SORT, LANES), 0).astype(jnp.float32)
 
     def sort(chunk, carry):
-        wanted = position + (chunk * LANES).astype(jnp.float32)
+        wanted = position + ((chunk * SORT).astype(jnp.float32) + 1.0)
 
         def add(part, accum):
-            hits = [
-                jnp.where(place_ref[part * step + k] == wanted, 1.0, 0.0).astype(jnp.bfloat16)
-                for k in range(step)
-            ]
+            hits = []
+            for k in range(step):
+                hits.append(jnp.where(place_ref[part * step + k] == wanted, 1.0, 0.0).astype(jnp.bfloat16))
             held = [payload_ref[part * step + k] for k in range(step)]
             return accum + lax.dot_general(
                 jnp.concatenate(held, axis=1),
@@ -179,15 +181,19 @@
                 preferred_element_type=jnp.float32,
             )
 
-        placed = joined(lax.fori_loop(0, parts, add, jnp.zeros((16, LANES), jnp.float32)))
-        feature_ref[chunk] = placed
-        time_ref[pl.ds(chunk, 1), :] = placed[3:4].astype(jnp.int32)
+        placed = joined(lax.fori_loop(0, parts, add, jnp.zeros((16, SORT), jnp.float32)))
+        time = placed[3:4].astype(jnp.int32)
+        begin = (time & (LANES - 1)) * (3 * chunks) + chunks - (time >> 7)
+        for k in range(SORT // LANES):
+            at = chunk * (SORT // LANES) + k
+            feature_ref[at] = placed[:, k * LANES : (k + 1) * LANES]
+            begin_ref[pl.ds(at, 1), :] = begin[:, k * LANES : (k + 1) * LANES]
         return carry
 
-    lax.fori_loop(0, filled, sort, 0)
-    feature_ref[filled] = jnp.zeros((4, LANES), jnp.float32)
-    time_copy = pltpu.make_async_copy(time_ref, time_smem, time_sem)
-    time_copy.start()
+    lax.fori_loop(0, (filled * LANES + SORT - 1) // SORT, sort, 0)
+    begin_copy = pltpu.make_async_copy(begin_ref, begin_smem, copy_sems.at[1])
+    begin_copy.start()
+    first_copy.wait()
 
     kernel = shaping_ref[...]
     lane, sublane = iota((chunks, LANES), 1), iota((chunks, LANES), 0)
@@ -199,21 +205,72 @@
         table_ref[base : base + chunks, :] = jnp.zeros((chunks, LANES), jnp.float32)
         table_ref[base + chunks : base + 2 * chunks, :] = pltpu.roll(jnp.where(inside, kernel, moved), shift, 1)
         table_ref[base + 2 * chunks : base + 3 * chunks, :] = pltpu.roll(jnp.where(inside, 0.0, tail), shift, 1)
-    time_copy.wait()
-    first_copy.wait()
+
+    spot, pad = iota((1, LANES), 1), iota((8, LANES), 0)
+    padded = -(-row_count // 8) * 8
+    row = iota((padded, LANES), 0)
+
+    def window_of(group, turn):
+        start, stop = first_smem[2 * group, 0], first_smem[2 * group + 3, 0]
+        begin = start // 16 * 16
+        limit = jnp.maximum((stop + LANES - 1) // LANES, 1) * LANES
+        wanted = begin + turn * LANES
+        return jnp.minimum(wanted, limit - LANES), wanted, (stop - begin + LANES - 1) // LANES, limit
+
+    def weights(group, turn):
+        begin, wanted, _, _ = window_of(group, turn)
+        chunk, offset = begin // LANES, begin % LANES
+        window = jnp.concatenate([feature_ref[chunk], feature_ref[chunk + 1]], axis=1)
+        window = pltpu.roll(jnp.concatenate([window, window], axis=0), 2 * LANES - offset, 1)[:, :LANES]
+        charge = jnp.where(spot < wanted - begin, 0.0, window[0:1])
+        below = window[1:2].astype(jnp.int32) - 1
+        beside = window[2:3].astype(jnp.int32) - (group * GROUP - 1) - pad
+        masks = [below == row + a for a in range(3)]
+        highs, lows = [], []
+        for a in range(3):
+            gain = jnp.where(
+                beside == 0,
+                response_ref[a, 0],
+                jnp.where(beside == 1, response_ref[a, 1], jnp.where(beside == 2, response_ref[a, 2], 0.0)),
+            )
+            term = charge * gain
+            high = term.astype(jnp.bfloat16).astype(jnp.float32)
+            highs.append(high)
+            lows.append(term - high)
+
+        def placed(terms):
+            blocks = []
+            for k in range(GROUP):
+                block = jnp.zeros((padded, LANES), jnp.float32)
+                for mask, term in zip(masks, terms):
+                    block = jnp.where(mask, term[k : k + 1], block)
+                blocks.append(block)
+            return jnp.concatenate(blocks, axis=0).astype(jnp.bfloat16)
+
+        return jnp.concatenate([placed(highs), placed(lows)], axis=1)
+
+    groups = PPR // GROUP
+
+    def weigh(part, carry):
+        for k in range(WEIGH):
+            group = part * WEIGH + k
+            weight_ref[group] = weights(group, 0)
+        return carry
+
+    lax.fori_loop(0, groups // WEIGH, weigh, 0)
+    begin_copy.wait()
 
     stride = stage_ref.shape[0] // chunks
 
     def shape(chunk, carry):
-        def eight(eighth, carry):
-            for k in range(8):
-                index = eighth * 8 + k
-                time = time_smem[chunk, index]
-                begin = (time & (LANES - 1)) * (3 * chunks) + chunks - (time >> 7)
+        def some(part, carry):
+            for k in range(ROWS):
+                index = part * ROWS + k
+                begin = begin_smem[chunk, index]
                 stage_ref[pl.ds(index, chunks, stride=stride), :] = table_ref[pl.ds(begin, chunks), :]
             return carry
 
-        lax.fori_loop(0, LANES // 8, eight, 0)
+        lax.fori_loop(0, LANES // ROWS, some, 0)
         at = pl.ds(pl.multiple_of(chunk * LANES, LANES), LANES)
         for c in range(chunks):
             value = stage_ref[c * stride : c * stride + LANES, :]
@@ -222,83 +279,62 @@
             low_ref[c, at, :] = (value - high.astype(jnp.float32)).astype(jnp.bfloat16)
         return carry
 
-    lax.fori_loop(0, filled, shape, 0)
-    beyond = pl.ds(pl.multiple_of(filled * LANES, LANES), LANES)
-    for c in range(chunks):
-        high_ref[c, beyond, :] = jnp.zeros((LANES, LANES), jnp.bfloat16)
-        low_ref[c, beyond, :] = jnp.zeros((LANES, LANES), jnp.bfloat16)
-
-    wide = 2 * LANES
-    spot = iota((1, wide), 1)
-    padded = -(-row_count // 8) * 8
-    row = iota((padded, wide), 0)
-
-    def weights(group, begin):
-        chunk, offset = begin // LANES, begin % LANES
-        window = jnp.concatenate([feature_ref[chunk], feature_ref[chunk + 1]], axis=1)
-        window = pltpu.roll(jnp.concatenate([window, window], axis=0), wide - offset, 1)
-        window = jnp.where(
-            spot < WINDOW,
-            window,
-            jnp.where(spot < 2 * WINDOW, pltpu.roll(window, WINDOW, 1), pltpu.roll(window, 2 * WINDOW, 1)),
+    def product(begin, c, held):
+        at = pl.ds(pl.multiple_of(begin, 16), LANES)
+        high = jnp.concatenate([high_ref[c, at, :], high_ref[c + 1, at, :]], axis=1)
+        low = jnp.concatenate([low_ref[c, at, :], low_ref[c + 1, at, :]], axis=1)
+        values = jnp.dot(
+            jnp.concatenate([held[:, :LANES], held], axis=1),
+            jnp.concatenate([low, high, high], axis=0),
+            preferred_element_type=jnp.float32,
         )
-        charge = jnp.where(spot < 3 * WINDOW, window[0:1], 0.0)
-        below, column = window[1:2].astype(jnp.int32) - 1 - row, window[2:3].astype(jnp.int32)
-        masks = [below == a for a in range(3)]
-        blocks = []
-        for k in range(GROUP):
-            beside = column - (group * GROUP + k - 1)
-            terms = []
-            for a in range(3):
-                gain = jnp.where(
-                    beside == 0,
-                    response_ref[a, 0],
-                    jnp.where(beside == 1, response_ref[a, 1], jnp.where(beside == 2, response_ref[a, 2], 0.0)),
-                )
-                term = charge * gain
-                high = term.astype(jnp.bfloat16).astype(jnp.float32)
-                terms.append(jnp.where(spot < 2 * WINDOW, high, term - high))
-            blocks.append(
-                jnp.where(masks[0], terms[0], jnp.where(masks[1], terms[1], jnp.where(masks[2], terms[2], 0.0)))
-            )
-        return jnp.concatenate(blocks, axis=0).astype(jnp.bfloat16)
-
-    def product(group, begin, c, held):
-        at = pl.ds(pl.multiple_of(begin, 16), WINDOW)
-        filler = jnp.zeros((wide - 3 * WINDOW, LANES), jnp.bfloat16)
-        high = [high_ref[k, at, :] for k in (c, c + 1)]
-        low = [low_ref[k, at, :] for k in (c, c + 1)]
-        columns = [jnp.concatenate([h, l, h, filler], axis=0) for h, l in zip(high, low)]
-        values = jnp.dot(held, jnp.concatenate(columns, axis=1), preferred_element_type=jnp.float32)
-        return values.reshape(GROUP, padded, wide)[:, :row_count]
-
-    def produce(group, carry):
-        start = first_smem[2 * group, 0]
-        stop = first_smem[2 * group + 3, 0]
-        begin = start // 16 * 16
+        return values.reshape(GROUP, padded, 2 * LANES)[:, :row_count]
+
+    def send(group):
         pads = pl.ds(group * GROUP, GROUP)
-        held = weights(group, begin)
-        for c in range(0, chunks, 2):
-            result_ref[pads, :, c * LANES : (c + 2) * LANES] = product(group, begin, c, held)
-
+        return pltpu.make_async_copy(result_ref.at[pads], out_ref.at[pads], out_sems.at[group])
+
+    def columns(group, c):
+        return pl.ds(group * GROUP, GROUP), slice(None), slice(c * LANES, (c + 2) * LANES)
+
+    def complete(group, carry):
         def more(turn, carry):
-            later = begin + turn * WINDOW
-            held = weights(group, later)
+            held = weights(group, turn)
             for c in range(0, chunks, 2):
-                at = (pads, slice(None), slice(c * LANES, (c + 2) * LANES))
-                result_ref[at] = result_ref[at] + product(group, later, c, held)
+                at = columns(group, c)
+                result_ref[at] = result_ref[at] + product(window_of(group, turn)[0], c, held)
             return carry
 
-        lax.fori_loop(1, (stop - begin + WINDOW - 1) // WINDOW, more, 0)
-        pltpu.make_async_copy(result_ref.at[pads], out_ref.at[pads], out_sems.at[group]).start()
+        lax.fori_loop(1, window_of(group, 0)[2], more, 0)
+        send(group).start()
         return carry
 
-    groups = PPR // GROUP
-    lax.fori_loop(0, groups, produce, 0)
+    shaped = 0
+    for batch in BATCHES:
+        places = [window_of(group, 0) for group in batch]
+        needed = places[-1][3] // LANES
+        lax.fori_loop(shaped, needed, shape, 0)
+        shaped = needed
+        most = functools.reduce(jnp.maximum, [windows for _, _, windows, _ in places])
+
+        def produce(group, begin):
+            for c in range(0, chunks, 2):
+                result_ref[columns(group, c)] = product(begin, c, weight_ref[group])
+
+        @pl.when(most <= 1)
+        def _():
+            for group, (begin, _, _, _) in zip(batch, places):
+                produce(group, begin)
+                send(group).start()
+
+        @pl.when(most > 1)
+        def _():
+            for group, (begin, _, _, _) in zip(batch, places):
+                produce(group, begin)
+            lax.fori_loop(batch[0], batch[-1] + 1, complete, 0)
 
     def finish(group, carry):
-        pads = pl.ds(group * GROUP, GROUP)
-        pltpu.make_async_copy(result_ref.at[pads], out_ref.at[pads], out_sems.at[group]).wait()
+        send(group).wait()
         return carry
 
     lax.fori_loop(0, groups, finish, 0)
@@ -309,7 +345,7 @@
     rows = charge.shape[1]
     capacity = max(16, 3 * rows // (2 * slabs))
     room = LANES // 2
-    assert capacity <= room and slabs % 2 == 0
+    assert capacity <= room and slabs % 2 == 0 and slabs * min(pads, 3) <= 256
     row_count = PROWS // pads
     vmem, smem = pl.BlockSpec(memory_space=pltpu.VMEM), pl.BlockSpec(memory_space=pltpu.SMEM)
     sources = (block_count, charge, pad_row, pad_column, time_bin, slab_owner.reshape(1, rows))
@@ -329,7 +365,7 @@
     count = slabs * pads
     step = min(count, 32)
     buckets = -(-(2 * PPR // GROUP + 2) // 8) * 8
-    most = -(-slabs * 2 * capacity * min(pads, 3) // LANES)
+    most = -(-slabs * 2 * capacity * min(pads, 3) // SORT) * (SORT // LANES)
     chunks = T_DEV // LANES
     stride = LANES + 8
     signal = pl.pallas_call(
@@ -343,22 +379,22 @@
             pltpu.VMEM((count * buckets, LANES), jnp.float32),
             pltpu.VMEM((step * buckets, 2 * LANES), jnp.float32),
             pltpu.VMEM((LANES * 3 * chunks, LANES), jnp.float32),
-            pltpu.VMEM((most + 2, 4, LANES), jnp.float32),
+            pltpu.VMEM((most + 1, 4, LANES), jnp.float32),
             pltpu.VMEM((most, LANES), jnp.int32),
             pltpu.VMEM((buckets, LANES), jnp.int32),
             pltpu.VMEM((chunks * stride, LANES), jnp.float32),
-            pltpu.VMEM((chunks, (most + 1) * LANES, LANES), jnp.bfloat16),
-            pltpu.VMEM((chunks, (most + 1) * LANES, LANES), jnp.bfloat16),
+            pltpu.VMEM((chunks, most * LANES, LANES), jnp.bfloat16),
+            pltpu.VMEM((chunks, most * LANES, LANES), jnp.bfloat16),
+            pltpu.VMEM((PPR // GROUP, GROUP * -(-row_count // 8) * 8, 2 * LANES), jnp.bfloat16),
             pltpu.VMEM((PPR, row_count, T_DEV), jnp.float32),
             pltpu.SMEM((most, LANES), jnp.int32),
             pltpu.SMEM((buckets, LANES), jnp.int32),
-            pltpu.SemaphoreType.DMA,
-            pltpu.SemaphoreType.DMA,
+            pltpu.SemaphoreType.DMA((2,)),
             pltpu.SemaphoreType.DMA((PPR // GROUP,)),
         ],
         compiler_params=pltpu.CompilerParams(vmem_limit_bytes=56 * 2**20),
         name="signal",
-    )(response, incoming, shaping.reshape(chunks, LANES))
+    )(response, pltpu.with_memory_space_constraint(incoming, pltpu.VMEM), pltpu.with_memory_space_constraint(shaping.reshape(chunks, LANES), pltpu.VMEM))
     return signal.transpose(1, 0, 2)
 
 

time: 33.6 us -> 24.7 us (0.74)
  the two profiles are of different devices: /device:TPU:4 before, /device:TPU:0 now
where the time goes in v1:
time: 24.7 us; the launch traced here: 24.3 us
  blocking collectives  14.5 us (59%)
  Pallas kernels  9.05 us (37%)
  local copies, waits for them, and re-layouts  0.69 us (3%)
    all_to_all x1, blocking collectives, body(): lax.all_to_all(outgoing, ('tm', 'pad'), split_axis=0, concat_axis=0, tile...  14.5 us
    pallas_call x1, Pallas kernels, body(): pl.pallas_call(functools.partial(signal_kernel, row_count), out_shape=jax...  7.62 us
    pallas_call x1, Pallas kernels, body(): pl.pallas_call(functools.partial(route_kernel, slabs, pads, row_count, ro...  1.43 us
    unnamed x2, local copies, waits for them, and re-layouts  0.69 us

profile of v1, /device:TPU:0, one launch (start us, length us, event | category | flops | bytes accessed | tf_op | source)
XLA Modules:
  0.0 24.3 jit_solution(5816345744901781997)
XLA Ops:
  0.0 1.4 %route.1 = f32[32,4,128]{2,1,0:T(4,128)S(1)} custom-call(s32[1]{0:T(128)} %bitcast.group_ref, s32[1,4]{1,0:T(1,128)} %refs_0_.1, f32[1,512]{1,0:T(1,128)} %refs_1_.1, s32[1,512]{1,0:T(1,128)} %refs_2_.1, s32[1,512]{1,0:T(1,128)} %refs_3_.1, s32[1,512]{1,0:T(1,128)} %refs_4_.1, s32[1,512]{1,0:T(1,128)} %bitcast.5), custom_call_target="tpu_custom_call" | custom-call | tf_op jit(solution)/shard_map/route/pallas_call | solution.py:353
  1.4 14.5 %all_to_all.5.slots_ref = f32[32,4,128]{2,1,0:T(4,128)S(1)} all-to-all(f32[32,4,128]{2,1,0:T(4,128)S(1)} %route.1), channel_id=1, replica_groups=mesh['tm'=16,'pad'=2] {'tm','pad'}, dimensions={0} | all-to-all | bytes 131072 | tf_op jit(solution)/shard_map/all_to_all | solution.py:363
  16.0 0.0 copy-start
  16.0 0.7 %copy-done = f32[1024]{0:T(1024)S(1)} copy-done((f32[1024]{0:T(1024)S(1)}, f32[1024]{0:T(1024)}, u32[]{:S(2)}) %copy-start) | copy-done | bytes 4120
  16.6 7.6 %signal.1 = f32[66,40,1024]{2,1,0:T(8,128)} custom-call(f32[3,3]{1,0:T(4,128)} %response_ref.1, f32[32,4,128]{2,1,0:T(4,128)S(1)} %all_to_all.5.slots_ref, f32[8,128]{1,0:T(8,128)S(1)} %bitcast.4), custom_call_target="tpu_custom_call" | custom-call | tf_op jit(solution)/shard_map/signal/pallas_call | solution.py:371
Async XLA Ops:
  16.0 0.7 %copy-start = (f32[1024]{0:T(1024)S(1)}, f32[1024]{0:T(1024)}, u32[]{:S(2)}) copy-start(f32[1024]{0:T(1024)} %param.14) | copy-start | bytes 12292

commit v2 on v1

--- a/solution.py
+++ b/solution.py
@@ -15,7 +15,6 @@
 GROUP = 6
 BATCHES = (range(0, 6), range(6, 11))
 WEIGH = 11
-ROWS = 128
 SORT = 256
 NT = (((1,), (1,)), ((), ()))
 
@@ -32,6 +31,10 @@
     return jnp.concatenate([high, middle, low, jnp.zeros_like(x)], axis=0).astype(jnp.bfloat16)
 
 
+def repeat(count, step, carry):
+    return step(0, carry) if count == 1 else lax.fori_loop(0, count, step, carry)
+
+
 def joined(x):
     return (x[0:4] + x[4:8]) + x[8:12]
 
@@ -41,17 +44,17 @@
     return jnp.where((lane >= LANES) | (source <= lane), 1.0, 0.0).astype(jnp.bfloat16)
 
 
-def route_kernel(slabs, pads, row_count, room, group_ref, *refs):
-    sources, (out_ref,), (sems,), targets = refs[:6], refs[6:7], refs[7:8], refs[8:]
+def route_kernel(slabs, pads, row_count, room, *refs):
+    sources, out_ref, sems, targets = refs[:7], refs[7], refs[9], (*refs[10:], refs[8])
     copies = [pltpu.make_async_copy(*pair, sems.at[k]) for k, pair in enumerate(zip(sources, targets))]
     for copy in copies:
         copy.start()
     for copy in copies:
         copy.wait()
-    count_ref, charge_ref, row_ref, column_ref, bin_ref, slab_ref = targets
+    count_ref, charge_ref, row_ref, column_ref, bin_ref, slab_ref, _ = targets
     rows = charge_ref.shape[1]
     blocks = rows // LANES
-    group = group_ref[0]
+    group = lax.axis_index("pad")
     sums = running()
     slab_ids = iota((slabs, LANES), 0)
     lane = iota((1, LANES), 1)
@@ -99,10 +102,11 @@
 
 def signal_kernel(
     row_count,
-    response_ref,
+    response_hbm,
     slots_ref,
     shaping_ref,
     out_ref,
+    response_ref,
     payload_ref,
     place_ref,
     marks_ref,
@@ -119,8 +123,11 @@
     begin_smem,
     first_smem,
     copy_sems,
+    begin_sems,
     out_sems,
 ):
+    response_copy = pltpu.make_async_copy(response_hbm, response_ref, copy_sems.at[1])
+    response_copy.start()
     count = slots_ref.shape[0]
     step = min(count, 32)
     parts = count // step
@@ -143,11 +150,22 @@
             earlier = earlier + jnp.where((bucket >= 0.0) & (bucket < bucket_ids), 1.0, 0.0)
         return earlier
 
-    earlier = lax.fori_loop(0, parts, mark, jnp.zeros((buckets, LANES), jnp.float32))
+    earlier = repeat(parts, mark, jnp.zeros((buckets, LANES), jnp.float32))
     first = jnp.dot(earlier.astype(jnp.bfloat16), sums, preferred_element_type=jnp.float32)[:, LANES:]
     first_ref[...] = first.astype(jnp.int32)
     first_copy = pltpu.make_async_copy(first_ref, first_smem, copy_sems.at[0])
     first_copy.start()
+
+    kernel = shaping_ref[...]
+    lane, sublane = iota((chunks, LANES), 1), iota((chunks, LANES), 0)
+    moved = jnp.concatenate([jnp.zeros((1, LANES), jnp.float32), kernel[: chunks - 1]], axis=0)
+    tail = jnp.where(sublane == 0, kernel[chunks - 1 : chunks], 0.0)
+    for shift in range(LANES):
+        inside = lane < LANES - shift
+        base = shift * 3 * chunks
+        table_ref[base : base + chunks, :] = jnp.zeros((chunks, LANES), jnp.float32)
+        table_ref[base + chunks : base + 2 * chunks, :] = pltpu.roll(jnp.where(inside, kernel, moved), shift, 1)
+        table_ref[base + 2 * chunks : base + 3 * chunks, :] = pltpu.roll(jnp.where(inside, 0.0, tail), shift, 1)
 
     def number(part, before):
         at = pl.ds(part * step * buckets, step * buckets)
@@ -160,7 +178,7 @@
             before = before + totals_ref[k * buckets : (k + 1) * buckets, LANES:]
         return before
 
-    lax.fori_loop(0, parts, number, first)
+    repeat(parts, number, first)
     total = jnp.max(first).astype(jnp.int32)
     filled = jnp.maximum((total + LANES - 1) // LANES, 1)
 
@@ -181,30 +199,27 @@
                 preferred_element_type=jnp.float32,
             )
 
-        placed = joined(lax.fori_loop(0, parts, add, jnp.zeros((16, SORT), jnp.float32)))
+        placed = joined(repeat(parts, add, jnp.zeros((16, SORT), jnp.float32)))
         time = placed[3:4].astype(jnp.int32)
         begin = (time & (LANES - 1)) * (3 * chunks) + chunks - (time >> 7)
         for k in range(SORT // LANES):
             at = chunk * (SORT // LANES) + k
             feature_ref[at] = placed[:, k * LANES : (k + 1) * LANES]
-            begin_ref[pl.ds(at, 1), :] = begin[:, k * LANES : (k + 1) * LANES]
+            begin_ref[chunk, pl.ds(k, 1), :] = begin[:, k * LANES : (k + 1) * LANES]
+        begins(chunk).start()
+        return carry
+
+    def begins(chunk):
+        at = pl.ds(chunk, 1)
+        return pltpu.make_async_copy(begin_ref.at[at], begin_smem.at[at], begin_sems.at[chunk])
+
+    def arrive(chunk, carry):
+        begins(chunk).wait()
         return carry
 
     lax.fori_loop(0, (filled * LANES + SORT - 1) // SORT, sort, 0)
-    begin_copy = pltpu.make_async_copy(begin_ref, begin_smem, copy_sems.at[1])
-    begin_copy.start()
     first_copy.wait()
-
-    kernel = shaping_ref[...]
-    lane, sublane = iota((chunks, LANES), 1), iota((chunks, LANES), 0)
-    moved = jnp.concatenate([jnp.zeros((1, LANES), jnp.float32), kernel[: chunks - 1]], axis=0)
-    tail = jnp.where(sublane == 0, kernel[chunks - 1 : chunks], 0.0)
-    for shift in range(LANES):
-        inside = lane < LANES - shift
-        base = shift * 3 * chunks
-        table_ref[base : base + chunks, :] = jnp.zeros((chunks, LANES), jnp.float32)
-        table_ref[base + chunks : base + 2 * chunks, :] = pltpu.roll(jnp.where(inside, kernel, moved), shift, 1)
-        table_ref[base + 2 * chunks : base + 3 * chunks, :] = pltpu.roll(jnp.where(inside, 0.0, tail), shift, 1)
+    response_copy.wait()
 
     spot, pad = iota((1, LANES), 1), iota((8, LANES), 0)
     padded = -(-row_count // 8) * 8
@@ -257,26 +272,22 @@
             weight_ref[group] = weights(group, 0)
         return carry
 
-    lax.fori_loop(0, groups // WEIGH, weigh, 0)
-    begin_copy.wait()
-
-    stride = stage_ref.shape[0] // chunks
-
-    def shape(chunk, carry):
-        def some(part, carry):
-            for k in range(ROWS):
-                index = part * ROWS + k
-                begin = begin_smem[chunk, index]
-                stage_ref[pl.ds(index, chunks, stride=stride), :] = table_ref[pl.ds(begin, chunks), :]
-            return carry
-
-        lax.fori_loop(0, LANES // ROWS, some, 0)
-        at = pl.ds(pl.multiple_of(chunk * LANES, LANES), LANES)
-        for c in range(chunks):
-            value = stage_ref[c * stride : c * stride + LANES, :]
-            high = value.astype(jnp.bfloat16)
-            high_ref[c, at, :] = high
-            low_ref[c, at, :] = (value - high.astype(jnp.float32)).astype(jnp.bfloat16)
+    repeat(groups // WEIGH, weigh, 0)
+
+    stride = stage_ref.shape[1] // chunks
+
+    def shape(pair, carry):
+        for half in range(SORT // LANES):
+            for k in range(LANES):
+                begin = begin_smem[pair, half, k]
+                stage_ref[half, pl.ds(k, chunks, stride=stride), :] = table_ref[pl.ds(begin, chunks), :]
+        for half in range(SORT // LANES):
+            at = pl.ds(pl.multiple_of(pair * SORT + half * LANES, LANES), LANES)
+            for c in range(chunks):
+                value = stage_ref[half, c * stride : c * stride + LANES, :]
+                high = value.astype(jnp.bfloat16)
+                high_ref[c, at, :] = high
+                low_ref[c, at, :] = (value - high.astype(jnp.float32)).astype(jnp.bfloat16)
         return carry
 
     def product(begin, c, held):
@@ -309,12 +320,16 @@
         send(group).start()
         return carry
 
-    shaped = 0
+    shaped, arrived = 0, 0
     for batch in BATCHES:
         places = [window_of(group, 0) for group in batch]
         needed = places[-1][3] // LANES
-        lax.fori_loop(shaped, needed, shape, 0)
-        shaped = needed
+        turns = (needed * LANES + SORT - 1) // SORT
+        if batch is BATCHES[-1]:
+            turns = (filled * LANES + SORT - 1) // SORT
+        lax.fori_loop(arrived, turns, arrive, 0)
+        lax.fori_loop(shaped, turns, shape, 0)
+        shaped, arrived = turns, turns
         most = functools.reduce(jnp.maximum, [windows for _, _, windows, _ in places])
 
         def produce(group, begin):
@@ -347,54 +362,59 @@
     room = LANES // 2
     assert capacity <= room and slabs % 2 == 0 and slabs * min(pads, 3) <= 256
     row_count = PROWS // pads
-    vmem, smem = pl.BlockSpec(memory_space=pltpu.VMEM), pl.BlockSpec(memory_space=pltpu.SMEM)
-    sources = (block_count, charge, pad_row, pad_column, time_bin, slab_owner.reshape(1, rows))
+    vmem = pl.BlockSpec(memory_space=pltpu.VMEM)
+    chunks = T_DEV // LANES
+    sources = (block_count, charge, pad_row, pad_column, time_bin, slab_owner.reshape(1, rows), shaping.reshape(chunks, LANES))
     sources = tuple(pltpu.with_memory_space_constraint(source, pltpu.HBM) for source in sources)
-    outgoing = pl.pallas_call(
+    outgoing, line = pl.pallas_call(
         functools.partial(route_kernel, slabs, pads, row_count, room),
-        out_shape=jax.ShapeDtypeStruct((slabs * pads, 4, LANES), jnp.float32),
-        in_specs=[smem] + [pl.BlockSpec(memory_space=pltpu.HBM)] * 6,
-        out_specs=vmem,
-        scratch_shapes=[pltpu.SemaphoreType.DMA((6,)), pltpu.SMEM(block_count.shape, block_count.dtype)]
-        + [pltpu.VMEM(source.shape, source.dtype) for source in sources[1:]],
+        out_shape=(
+            jax.ShapeDtypeStruct((slabs * pads, 4, LANES), jnp.float32),
+            jax.ShapeDtypeStruct((chunks, LANES), jnp.float32),
+        ),
+        in_specs=[pl.BlockSpec(memory_space=pltpu.HBM)] * 7,
+        out_specs=(vmem, vmem),
+        scratch_shapes=[pltpu.SemaphoreType.DMA((7,)), pltpu.SMEM(block_count.shape, block_count.dtype)]
+        + [pltpu.VMEM(source.shape, source.dtype) for source in sources[1:6]],
         compiler_params=pltpu.CompilerParams(vmem_limit_bytes=32 * 2**20),
         name="route",
-    )(lax.axis_index("pad").astype(jnp.int32).reshape(1), *sources)
+    )(*sources)
     incoming = lax.all_to_all(outgoing, ("tm", "pad"), split_axis=0, concat_axis=0, tiled=True)
 
     count = slabs * pads
     step = min(count, 32)
     buckets = -(-(2 * PPR // GROUP + 2) // 8) * 8
     most = -(-slabs * 2 * capacity * min(pads, 3) // SORT) * (SORT // LANES)
-    chunks = T_DEV // LANES
-    stride = LANES + 8
+    stride = LANES + 4
     signal = pl.pallas_call(
         functools.partial(signal_kernel, row_count),
         out_shape=jax.ShapeDtypeStruct((PPR, row_count, T_DEV), jnp.float32),
-        in_specs=[smem, vmem, vmem],
+        in_specs=[pl.BlockSpec(memory_space=pltpu.HBM), vmem, vmem],
         out_specs=pl.BlockSpec(memory_space=pl.ANY),
         scratch_shapes=[
+            pltpu.SMEM(response.shape, response.dtype),
             pltpu.VMEM((count, 16, LANES), jnp.bfloat16),
             pltpu.VMEM((count, 1, LANES), jnp.float32),
             pltpu.VMEM((count * buckets, LANES), jnp.float32),
             pltpu.VMEM((step * buckets, 2 * LANES), jnp.float32),
             pltpu.VMEM((LANES * 3 * chunks, LANES), jnp.float32),
             pltpu.VMEM((most + 1, 4, LANES), jnp.float32),
-            pltpu.VMEM((most, LANES), jnp.int32),
+            pltpu.VMEM((most * LANES // SORT, SORT // LANES, LANES), jnp.int32),
             pltpu.VMEM((buckets, LANES), jnp.int32),
-            pltpu.VMEM((chunks * stride, LANES), jnp.float32),
+            pltpu.VMEM((SORT // LANES, chunks * stride, LANES), jnp.float32),
             pltpu.VMEM((chunks, most * LANES, LANES), jnp.bfloat16),
             pltpu.VMEM((chunks, most * LANES, LANES), jnp.bfloat16),
             pltpu.VMEM((PPR // GROUP, GROUP * -(-row_count // 8) * 8, 2 * LANES), jnp.bfloat16),
             pltpu.VMEM((PPR, row_count, T_DEV), jnp.float32),
-            pltpu.SMEM((most, LANES), jnp.int32),
+            pltpu.SMEM((most * LANES // SORT, SORT // LANES, LANES), jnp.int32),
             pltpu.SMEM((buckets, LANES), jnp.int32),
             pltpu.SemaphoreType.DMA((2,)),
+            pltpu.SemaphoreType.DMA((most * LANES // SORT,)),
             pltpu.SemaphoreType.DMA((PPR // GROUP,)),
         ],
         compiler_params=pltpu.CompilerParams(vmem_limit_bytes=56 * 2**20),
         name="signal",
-    )(response, pltpu.with_memory_space_constraint(incoming, pltpu.VMEM), pltpu.with_memory_space_constraint(shaping.reshape(chunks, LANES), pltpu.VMEM))
+    )(pltpu.with_memory_space_constraint(response, pltpu.HBM), pltpu.with_memory_space_constraint(incoming, pltpu.VMEM), pltpu.with_memory_space_constraint(line, pltpu.VMEM))
     return signal.transpose(1, 0, 2)
 
 

time: 24.7 us -> 23.9 us (0.968)
  the two profiles are of different devices: /device:TPU:0 before, /device:TPU:1 now
where the time goes in v2:
time: 23.9 us; the launch traced here: 23.5 us
  blocking collectives  14.2 us (59%)
  Pallas kernels  9.33 us (39%)
    all_to_all x1, blocking collectives, body(): lax.all_to_all(outgoing, ('tm', 'pad'), split_axis=0, concat_axis=0, tile...  14.2 us
    pallas_call x1, Pallas kernels, body(): pl.pallas_call(functools.partial(signal_kernel, row_count), out_shape=jax...  7.87 us
    pallas_call x1, Pallas kernels, body(): pl.pallas_call(functools.partial(route_kernel, slabs, pads, row_count, ro...  1.46 us

profile of v2, /device:TPU:1, one launch (start us, length us, event | category | flops | bytes accessed | tf_op | source)
XLA Modules:
  0.0 23.5 jit_solution(1595397882042858855)
XLA Ops:
  0.0 1.5 %route.1 = (f32[32,4,128]{2,1,0:T(4,128)S(1)}, f32[8,128]{1,0:T(8,128)S(1)}) custom-call(s32[1,4]{1,0:T(1,128)} %refs_0_.1, f32[1,512]{1,0:T(1,128)} %refs_1_.1, s32[1,512]{1,0:T(1,128)} %refs_2_.1, s32[1,512]{1,0:T(1,128)} %refs_3_.1, s32[1,512]{1,0:T(1,128)} %refs_4_.1, s32[1,512]{1,0:T(1,128)} %bitcast.4, f32[8,128]{1,0:T(8,128)} %bitcast.3), custom_call_target="tpu_custom_call" | custom-call | tf_op jit(solution)/shard_map/route/pallas_call | solution.py:369
  1.5 14.2 %all_to_all.5.slots_ref = f32[32,4,128]{2,1,0:T(4,128)S(1)} all-to-all(f32[32,4,128]{2,1,0:T(4,128)S(1)} %get-tuple-element.7), channel_id=1, replica_groups=mesh['tm'=16,'pad'=2] {'tm','pad'}, dimensions={0} | all-to-all | bytes 131072 | tf_op jit(solution)/shard_map/all_to_all | solution.py:382
  15.6 7.9 %signal.1 = f32[66,40,1024]{2,1,0:T(8,128)} custom-call(f32[3,3]{1,0:T(4,128)} %response_hbm.1, f32[32,4,128]{2,1,0:T(4,128)S(1)} %all_to_all.5.slots_ref, f32[8,128]{1,0:T(8,128)S(1)} %get-tuple-element.8.shaping_ref), custom_call_target="tpu_custom_call" | custom-call | tf_op jit(solution)/shard_map/signal/pallas_call | solution.py:389

commit v3 on v2

--- a/solution.py
+++ b/solution.py
@@ -15,7 +15,7 @@
 GROUP = 6
 BATCHES = (range(0, 6), range(6, 11))
 WEIGH = 11
-SORT = 256
+SORT = 1024
 NT = (((1,), (1,)), ((), ()))
 
 
@@ -23,12 +23,11 @@
     return lax.broadcasted_iota(jnp.int32, shape, dim)
 
 
-def pieces(x):
+def thirds(x):
     high = x.astype(jnp.bfloat16).astype(jnp.float32)
     rest = x - high
     middle = rest.astype(jnp.bfloat16).astype(jnp.float32)
-    low = rest - middle
-    return jnp.concatenate([high, middle, low, jnp.zeros_like(x)], axis=0).astype(jnp.bfloat16)
+    return high, middle, rest - middle
 
 
 def repeat(count, step, carry):
@@ -56,10 +55,11 @@
     blocks = rows // LANES
     group = lax.axis_index("pad")
     sums = running()
-    slab_ids = iota((slabs, LANES), 0)
+    slab_ids, row_slabs = iota((slabs, LANES), 0), iota((4 * slabs, LANES), 0) // 4
     lane = iota((1, LANES), 1)
+    wanted = (iota((LANES, LANES), 0) % room + 1).astype(jnp.float32)
     before = jnp.zeros((slabs, LANES), jnp.float32)
-    slots, values = [], []
+    rows_of, hits = [], []
     for block in range(blocks):
         at = pl.ds(block * LANES, LANES)
         live = lane < count_ref[0, block]
@@ -68,36 +68,36 @@
         totals = jnp.dot(marks.astype(jnp.bfloat16), sums, preferred_element_type=jnp.float32)
         rank = jnp.sum(marks * (totals[:, :LANES] + before), axis=0, keepdims=True)
         before = before + totals[:, LANES:]
-        slots.append(jnp.where(live, slab * room + rank.astype(jnp.int32) - 1, -1))
-        values.append(
-            jnp.concatenate(
-                [
-                    charge_ref[:, at],
-                    (row_ref[:, at] + 2).astype(jnp.float32),
-                    column_ref[:, at].astype(jnp.float32),
-                    bin_ref[:, at].astype(jnp.float32),
-                ],
-                axis=0,
-            )
+        hits.append(jnp.where(wanted == rank, 1.0, 0.0).astype(jnp.bfloat16))
+        value = jnp.concatenate(
+            [
+                charge_ref[:, at],
+                (row_ref[:, at] + 2).astype(jnp.float32),
+                column_ref[:, at].astype(jnp.float32),
+                bin_ref[:, at].astype(jnp.float32),
+            ],
+            axis=0,
         )
-    payload = pieces(jnp.concatenate(values, axis=1))
-    slot = jnp.concatenate(slots, axis=1)
-    hits = jnp.where(iota((slabs * room, rows), 0) == slot, 1.0, 0.0).astype(jnp.bfloat16)
-    placed = joined(lax.dot_general(payload, hits, NT, preferred_element_type=jnp.float32))
-    feature, half = iota((4, LANES), 0), iota((4, LANES), 1) // room
-    for slab in range(slabs):
-        tile = placed[:, slab // 2 * LANES : slab // 2 * LANES + LANES]
-        if slab % 2 == 0:
-            other = placed[:, (slab // 2 - 1) * LANES : slab // 2 * LANES] if slab else jnp.zeros_like(tile)
-            tile = jnp.where(half == 0, tile, other)
-        tile = jnp.where((feature == 3) & (half != slab % 2), tile - T_DEV, tile)
-        top = jnp.where(feature == 1, jnp.where(tile == row_count + 1, 1.0, 0.0), tile)
-        bottom = jnp.where(feature == 1, jnp.where(tile == 2, row_count + 2.0, 0.0), tile)
-        for pad in range(pads):
-            apart = pad - group
-            out_ref[slab * pads + pad] = jnp.where(
-                apart == 0, tile, jnp.where(apart == 1, top, jnp.where(apart == -1, bottom, 0.0))
-            )
+        here = row_slabs == slab
+        terms = []
+        for term in thirds(jnp.concatenate([value, value], axis=0)):
+            terms.append(jnp.where(here, jnp.concatenate([term] * (slabs // 2), axis=0), 0.0))
+        rows_of.append(jnp.concatenate(terms, axis=0).astype(jnp.bfloat16))
+    sent = lax.dot_general(
+        jnp.concatenate(rows_of, axis=1), jnp.concatenate(hits, axis=1), NT, preferred_element_type=jnp.float32
+    )
+    sent = (sent[: 4 * slabs] + sent[4 * slabs : 8 * slabs]) + sent[8 * slabs :]
+    earlier = jnp.concatenate([jnp.zeros((4, LANES), jnp.float32), sent[:-4]], axis=0)
+    feature, late = iota((4 * slabs, LANES), 0) % 4, iota((4 * slabs, LANES), 1) >= room
+    sent = jnp.where(late, earlier, sent)
+    sent = jnp.where((feature == 3) & late, sent - T_DEV, sent)
+    top = jnp.where(feature == 1, jnp.where(sent == row_count + 1, 1.0, 0.0), sent)
+    bottom = jnp.where(feature == 1, jnp.where(sent == 2, row_count + 2.0, 0.0), sent)
+    for pad in range(pads):
+        apart = pad - group
+        chosen = jnp.where(apart == 0, sent, jnp.where(apart == 1, top, jnp.where(apart == -1, bottom, 0.0)))
+        for slab in range(slabs):
+            out_ref[slab * pads + pad] = chosen[4 * slab : 4 * slab + 4]
 
 
 def signal_kernel(
@@ -141,7 +141,7 @@
         for k in range(step):
             block = part * step + k
             slot = slots_ref[block]
-            payload_ref[block] = pieces(slot)
+            payload_ref[block] = jnp.concatenate([*thirds(slot), jnp.zeros_like(slot)], axis=0)
             column = slot[2:3] + 1.0
             group = jnp.floor((column + 0.5) * (1.0 / GROUP))
             inside = jnp.where(column - group * GROUP > 1.5, 1.0, 0.0)
@@ -182,16 +182,20 @@
     total = jnp.max(first).astype(jnp.int32)
     filled = jnp.maximum((total + LANES - 1) // LANES, 1)
 
-    position = iota((SORT, LANES), 0).astype(jnp.float32)
-
-    def sort(chunk, carry):
-        wanted = position + ((chunk * SORT).astype(jnp.float32) + 1.0)
+    position = iota((LANES, LANES), 0).astype(jnp.float32)
+
+    def sort(turn, carry):
+        base = (turn * SORT).astype(jnp.float32) + 1.0
 
         def add(part, accum):
-            hits = []
+            hits, held = [], []
             for k in range(step):
-                hits.append(jnp.where(place_ref[part * step + k] == wanted, 1.0, 0.0).astype(jnp.bfloat16))
-            held = [payload_ref[part * step + k] for k in range(step)]
+                place = place_ref[part * step + k] - base
+                chunk = jnp.floor(place * (1.0 / LANES))
+                hits.append(jnp.where(place - chunk * LANES == position, 1.0, 0.0).astype(jnp.bfloat16))
+                payload = payload_ref[part * step + k]
+                rows = [jnp.where(chunk == c, payload, 0.0) for c in range(SORT // LANES)]
+                held.append(jnp.concatenate(rows, axis=0).astype(jnp.bfloat16))
             return accum + lax.dot_general(
                 jnp.concatenate(held, axis=1),
                 jnp.concatenate(hits, axis=1),
@@ -199,25 +203,25 @@
                 preferred_element_type=jnp.float32,
             )
 
-        placed = joined(repeat(parts, add, jnp.zeros((16, SORT), jnp.float32)))
-        time = placed[3:4].astype(jnp.int32)
-        begin = (time & (LANES - 1)) * (3 * chunks) + chunks - (time >> 7)
+        placed = repeat(parts, add, jnp.zeros((16 * SORT // LANES, LANES), jnp.float32))
         for k in range(SORT // LANES):
-            at = chunk * (SORT // LANES) + k
-            feature_ref[at] = placed[:, k * LANES : (k + 1) * LANES]
-            begin_ref[chunk, pl.ds(k, 1), :] = begin[:, k * LANES : (k + 1) * LANES]
-        begins(chunk).start()
-        return carry
-
-    def begins(chunk):
-        at = pl.ds(chunk, 1)
-        return pltpu.make_async_copy(begin_ref.at[at], begin_smem.at[at], begin_sems.at[chunk])
-
-    def arrive(chunk, carry):
-        begins(chunk).wait()
-        return carry
-
-    lax.fori_loop(0, (filled * LANES + SORT - 1) // SORT, sort, 0)
+            features = joined(placed[16 * k : 16 * k + 16])
+            feature_ref[turn * (SORT // LANES) + k] = features
+            time = features[3:4].astype(jnp.int32)
+            begin_ref[turn, pl.ds(k, 1), :] = (time & (LANES - 1)) * (3 * chunks) + chunks - (time >> 7)
+        begins(turn).start()
+        return carry
+
+    def begins(turn):
+        at = pl.ds(turn, 1)
+        return pltpu.make_async_copy(begin_ref.at[at], begin_smem.at[at], begin_sems.at[turn])
+
+    def arrive(turn, carry):
+        begins(turn).wait()
+        return carry
+
+    turns = (filled * LANES + SORT - 1) // SORT
+    lax.fori_loop(0, turns, sort, 0)
     first_copy.wait()
     response_copy.wait()
 
@@ -274,15 +278,18 @@
 
     repeat(groups // WEIGH, weigh, 0)
 
+    lax.fori_loop(0, turns, arrive, 0)
+
     stride = stage_ref.shape[1] // chunks
 
     def shape(pair, carry):
-        for half in range(SORT // LANES):
+        for half in range(2):
+            chunk = pair * 2 + half
             for k in range(LANES):
-                begin = begin_smem[pair, half, k]
+                begin = begin_smem[chunk // (SORT // LANES), chunk % (SORT // LANES), k]
                 stage_ref[half, pl.ds(k, chunks, stride=stride), :] = table_ref[pl.ds(begin, chunks), :]
-        for half in range(SORT // LANES):
-            at = pl.ds(pl.multiple_of(pair * SORT + half * LANES, LANES), LANES)
+        for half in range(2):
+            at = pl.ds(pl.multiple_of((pair * 2 + half) * LANES, LANES), LANES)
             for c in range(chunks):
                 value = stage_ref[half, c * stride : c * stride + LANES, :]
                 high = value.astype(jnp.bfloat16)
@@ -320,16 +327,12 @@
         send(group).start()
         return carry
 
-    shaped, arrived = 0, 0
+    shaped = 0
     for batch in BATCHES:
         places = [window_of(group, 0) for group in batch]
         needed = places[-1][3] // LANES
-        turns = (needed * LANES + SORT - 1) // SORT
-        if batch is BATCHES[-1]:
-            turns = (filled * LANES + SORT - 1) // SORT
-        lax.fori_loop(arrived, turns, arrive, 0)
-        lax.fori_loop(shaped, turns, shape, 0)
-        shaped, arrived = turns, turns
+        lax.fori_loop(shaped, (needed + 1) // 2, shape, 0)
+        shaped = (needed + 1) // 2
         most = functools.reduce(jnp.maximum, [windows for _, _, windows, _ in places])
 
         def produce(group, begin):
@@ -393,7 +396,7 @@
         out_specs=pl.BlockSpec(memory_space=pl.ANY),
         scratch_shapes=[
             pltpu.SMEM(response.shape, response.dtype),
-            pltpu.VMEM((count, 16, LANES), jnp.bfloat16),
+            pltpu.VMEM((count, 16, LANES), jnp.float32),
             pltpu.VMEM((count, 1, LANES), jnp.float32),
             pltpu.VMEM((count * buckets, LANES), jnp.float32),
             pltpu.VMEM((step * buckets, 2 * LANES), jnp.float32),
@@ -401,7 +404,7 @@
             pltpu.VMEM((most + 1, 4, LANES), jnp.float32),
             pltpu.VMEM((most * LANES // SORT, SORT // LANES, LANES), jnp.int32),
             pltpu.VMEM((buckets, LANES), jnp.int32),
-            pltpu.VMEM((SORT // LANES, chunks * stride, LANES), jnp.float32),
+            pltpu.VMEM((2, chunks * stride, LANES), jnp.float32),
             pltpu.VMEM((chunks, most * LANES, LANES), jnp.bfloat16),
             pltpu.VMEM((chunks, most * LANES, LANES), jnp.bfloat16),
             pltpu.VMEM((PPR // GROUP, GROUP * -(-row_count // 8) * 8, 2 * LANES), jnp.bfloat16),

time: 23.9 us -> 23.1 us (0.967)
  the two profiles are of different devices: /device:TPU:1 before, /device:TPU:0 now
where the time goes in v3:
time: 23.1 us; the launch traced here: 22.9 us
  blocking collectives  14.5 us (63%)
  Pallas kernels  8.34 us (36%)
    all_to_all x1, blocking collectives, body(): lax.all_to_all(outgoing, ('tm', 'pad'), split_axis=0, concat_axis=0, tile...  14.5 us
    pallas_call x1, Pallas kernels, body(): pl.pallas_call(functools.partial(signal_kernel, row_count), out_shape=jax...  7.13 us
    pallas_call x1, Pallas kernels, body(): pl.pallas_call(functools.partial(route_kernel, slabs, pads, row_count, ro...  1.2 us

profile of v3, /device:TPU:0, one launch (start us, length us, event | category | flops | bytes accessed | tf_op | source)
XLA Modules:
  0.0 22.9 jit_solution(15473808873627241730)
XLA Ops:
  0.0 1.2 %route.1 = (f32[32,4,128]{2,1,0:T(4,128)S(1)}, f32[8,128]{1,0:T(8,128)S(1)}) custom-call(s32[1,4]{1,0:T(1,128)} %refs_0_.1, f32[1,512]{1,0:T(1,128)} %refs_1_.1, s32[1,512]{1,0:T(1,128)} %refs_2_.1, s32[1,512]{1,0:T(1,128)} %refs_3_.1, s32[1,512]{1,0:T(1,128)} %refs_4_.1, s32[1,512]{1,0:T(1,128)} %bitcast.4, f32[8,128]{1,0:T(8,128)} %bitcast.3), custom_call_target="tpu_custom_call" | custom-call | tf_op jit(solution)/shard_map/route/pallas_call | solution.py:372
  1.2 14.5 %all_to_all.5.slots_ref = f32[32,4,128]{2,1,0:T(4,128)S(1)} all-to-all(f32[32,4,128]{2,1,0:T(4,128)S(1)} %get-tuple-element.7), channel_id=1, replica_groups=mesh['tm'=16,'pad'=2] {'tm','pad'}, dimensions={0} | all-to-all | bytes 131072 | tf_op jit(solution)/shard_map/all_to_all | solution.py:385
  15.7 7.1 %signal.1 = f32[66,40,1024]{2,1,0:T(8,128)} custom-call(f32[3,3]{1,0:T(4,128)} %response_hbm.1, f32[32,4,128]{2,1,0:T(4,128)S(1)} %all_to_all.5.slots_ref, f32[8,128]{1,0:T(8,128)S(1)} %get-tuple-element.8.shaping_ref), custom_call_target="tpu_custom_call" | custom-call | tf_op jit(solution)/shard_map/signal/pallas_call | solution.py:392

commit v4 on v3

--- a/solution.py
+++ b/solution.py
@@ -14,7 +14,6 @@
 LANES = 128
 GROUP = 6
 BATCHES = (range(0, 6), range(6, 11))
-WEIGH = 11
 SORT = 1024
 NT = (((1,), (1,)), ((), ()))
 
@@ -156,17 +155,6 @@
     first_copy = pltpu.make_async_copy(first_ref, first_smem, copy_sems.at[0])
     first_copy.start()
 
-    kernel = shaping_ref[...]
-    lane, sublane = iota((chunks, LANES), 1), iota((chunks, LANES), 0)
-    moved = jnp.concatenate([jnp.zeros((1, LANES), jnp.float32), kernel[: chunks - 1]], axis=0)
-    tail = jnp.where(sublane == 0, kernel[chunks - 1 : chunks], 0.0)
-    for shift in range(LANES):
-        inside = lane < LANES - shift
-        base = shift * 3 * chunks
-        table_ref[base : base + chunks, :] = jnp.zeros((chunks, LANES), jnp.float32)
-        table_ref[base + chunks : base + 2 * chunks, :] = pltpu.roll(jnp.where(inside, kernel, moved), shift, 1)
-        table_ref[base + 2 * chunks : base + 3 * chunks, :] = pltpu.roll(jnp.where(inside, 0.0, tail), shift, 1)
-
     def number(part, before):
         at = pl.ds(part * step * buckets, step * buckets)
         totals_ref[...] = jnp.dot(marks_ref[at, :].astype(jnp.bfloat16), sums, preferred_element_type=jnp.float32)
@@ -224,6 +212,17 @@
     lax.fori_loop(0, turns, sort, 0)
     first_copy.wait()
     response_copy.wait()
+
+    kernel = shaping_ref[...]
+    lane, sublane = iota((chunks, LANES), 1), iota((chunks, LANES), 0)
+    moved = jnp.concatenate([jnp.zeros((1, LANES), jnp.float32), kernel[: chunks - 1]], axis=0)
+    tail = jnp.where(sublane == 0, kernel[chunks - 1 : chunks], 0.0)
+    for shift in range(LANES):
+        inside = lane < LANES - shift
+        base = shift * 3 * chunks
+        table_ref[base : base + chunks, :] = jnp.zeros((chunks, LANES), jnp.float32)
+        table_ref[base + chunks : base + 2 * chunks, :] = pltpu.roll(jnp.where(inside, kernel, moved), shift, 1)
+        table_ref[base + 2 * chunks : base + 3 * chunks, :] = pltpu.roll(jnp.where(inside, 0.0, tail), shift, 1)
 
     spot, pad = iota((1, LANES), 1), iota((8, LANES), 0)
     padded = -(-row_count // 8) * 8
@@ -270,13 +269,6 @@
 
     groups = PPR // GROUP
 
-    def weigh(part, carry):
-        for k in range(WEIGH):
-            group = part * WEIGH + k
-            weight_ref[group] = weights(group, 0)
-        return carry
-
-    repeat(groups // WEIGH, weigh, 0)
 
     lax.fori_loop(0, turns, arrive, 0)
 
@@ -341,12 +333,16 @@
 
         @pl.when(most <= 1)
         def _():
+            for group in batch:
+                weight_ref[group] = weights(group, 0)
             for group, (begin, _, _, _) in zip(batch, places):
                 produce(group, begin)
                 send(group).start()
 
         @pl.when(most > 1)
         def _():
+            for group in batch:
+                weight_ref[group] = weights(group, 0)
             for group, (begin, _, _, _) in zip(batch, places):
                 produce(group, begin)
             lax.fori_loop(batch[0], batch[-1] + 1, complete, 0)

time: 23.1 us -> 22.6 us (0.978)
  Pallas kernels: 8.34 us -> 7.9 us
    pallas_call x1, Pallas kernels: 7.13 us -> 6.69 us  [body(): pl.pallas_call(functools.partial(signal_kernel, row_count), out_shape=jax...]
where the time goes in v4:
time: 22.6 us; the launch traced here: 22.4 us
  blocking collectives  14.5 us (64%)
  Pallas kernels  7.9 us (35%)
    all_to_all x1, blocking collectives, body(): lax.all_to_all(outgoing, ('tm', 'pad'), split_axis=0, concat_axis=0, tile...  14.5 us
    pallas_call x1, Pallas kernels, body(): pl.pallas_call(functools.partial(signal_kernel, row_count), out_shape=jax...  6.69 us
    pallas_call x1, Pallas kernels, body(): pl.pallas_call(functools.partial(route_kernel, slabs, pads, row_count, ro...  1.2 us

profile of v4, /device:TPU:0, one launch (start us, length us, event | category | flops | bytes accessed | tf_op | source)
XLA Modules:
  0.0 22.4 jit_solution(3461719918299559141)
XLA Ops:
  0.0 1.2 %route.1 = (f32[32,4,128]{2,1,0:T(4,128)S(1)}, f32[8,128]{1,0:T(8,128)S(1)}) custom-call(s32[1,4]{1,0:T(1,128)} %refs_0_.1, f32[1,512]{1,0:T(1,128)} %refs_1_.1, s32[1,512]{1,0:T(1,128)} %refs_2_.1, s32[1,512]{1,0:T(1,128)} %refs_3_.1, s32[1,512]{1,0:T(1,128)} %refs_4_.1, s32[1,512]{1,0:T(1,128)} %bitcast.4, f32[8,128]{1,0:T(8,128)} %bitcast.3), custom_call_target="tpu_custom_call" | custom-call | tf_op jit(solution)/shard_map/route/pallas_call | solution.py:368
  1.2 14.5 %all_to_all.5.slots_ref = f32[32,4,128]{2,1,0:T(4,128)S(1)} all-to-all(f32[32,4,128]{2,1,0:T(4,128)S(1)} %get-tuple-element.7), channel_id=1, replica_groups=mesh['tm'=16,'pad'=2] {'tm','pad'}, dimensions={0} | all-to-all | bytes 131072 | tf_op jit(solution)/shard_map/all_to_all | solution.py:381
  15.7 6.7 %signal.1 = f32[66,40,1024]{2,1,0:T(8,128)} custom-call(f32[3,3]{1,0:T(4,128)} %response_hbm.1, f32[32,4,128]{2,1,0:T(4,128)S(1)} %all_to_all.5.slots_ref, f32[8,128]{1,0:T(8,128)S(1)} %get-tuple-element.8.shaping_ref), custom_call_target="tpu_custom_call" | custom-call | tf_op jit(solution)/shard_map/signal/pallas_call | solution.py:388
